TPU v7x, 32 devices: a whole 2x2x4 slice. The times are simulated.
32 devices in a mesh: pair: 8 (over z, x), cores: 2 (over core), split: 2 (over y).
Axes of the slice: x: 2, y: 2, z: 4, core: 2. Of those that a mesh axis runs over, the one named last changes fastest.
Arguments:
- summand_cores: float32 [8, 2, 128, 16, 128], P('pair', 'cores', None, 'split'), may hold values from -0.088388348 to 0.088388348
- sketch_cores: bfloat16 [2, 128, 16, 128], P('cores', None, 'split'), may hold values from -0.5 to 0.5
Outputs:
- rounded_cores: float32 [8, 2, 128, 16, 128], P('pair', 'cores', None, 'split')
All inputs are finite; a program needn't handle non-finite values.
Results may differ from a plain program's by a relative error of at most 0.00035.
Values sent between devices are 32-bit elements; how exact they have to be, the bound alone decides.
A program may use at most 64 MiB of HBM per device.

v0:
```python
import jax
import jax.numpy as jnp
from jax import lax
from jax.sharding import PartitionSpec as P

RANK = 128


highest = lax.Precision.HIGHEST
shift_ratio = 0.01


def passed_along(block, axis, distance):
    devices = range(lax.axis_size(axis))
    route = [(i - distance, i) for i in devices if i - distance in devices]
    return lax.ppermute(block, axis, route)


def shifted_2(value, axis, steps):
    count = lax.axis_size(axis)
    pairs = [(source, (source + steps) % count) for source in range(count)]
    return lax.ppermute(value, axis, pairs)


def contract_sketch(own_core, sketch_in, sketch_core):
    inner = jnp.einsum("aib,bm->aim", own_core, sketch_in, precision=highest)
    return jnp.einsum("aim,lim->al", inner, sketch_core, precision=highest)


def body(summand_cores, sketch_cores):
    own_core = summand_cores[0, 0]
    sketch_core = sketch_cores[0].astype(jnp.float32)
    rank_dim = own_core.shape[0]
    train_depth = lax.axis_size("cores")
    core_place = lax.axis_index("cores")
    mode_size = own_core.shape[1] * lax.axis_size("split")
    out_scale = (RANK * mode_size) ** 0.5
    identity = jnp.eye(rank_dim, dtype=jnp.float32)
    zero_square = jnp.zeros((rank_dim, rank_dim), jnp.float32)
    zero_block = jnp.zeros(own_core.shape, jnp.float32)
    stride = lax.axis_size("pair") // 4

    def sketch_turn(step_index, carry_state):
        own_sketch, next_sketch = carry_state
        arrived = passed_along(own_sketch, "cores", -1)
        active = core_place == train_depth - 1 - step_index
        sketch_in = jnp.where(core_place == train_depth - 1, identity, arrived)
        partial_value = lax.cond(
            active, lambda: contract_sketch(own_core, sketch_in, sketch_core), lambda: zero_square
        )
        summed = lax.psum(partial_value, "split")
        own_sketch = jnp.where(active, summed, own_sketch)
        next_sketch = jnp.where(active, sketch_in, next_sketch)
        return (own_sketch, next_sketch)

    own_sketch, next_sketch = lax.fori_loop(0, train_depth, sketch_turn, (zero_square, zero_square))
    other_core, other_sketch = shifted_2((own_core, next_sketch), "pair", -stride)
    joined = jnp.concatenate([identity, identity], axis=1)

    def carry_turn(step_index, carry_state):
        own_carry, result = carry_state
        arrived = passed_along(own_carry, "cores", 1)
        carry_in = jnp.where(core_place == 0, joined, arrived)
        active = core_place == step_index
        is_last = core_place == train_depth - 1

        def heavy_work():
            moved_own = jnp.einsum(
                "la,aib->lib", carry_in[:, :rank_dim], own_core, precision=highest
            )
            moved_other = jnp.einsum(
                "la,aib->lib", carry_in[:, rank_dim:], other_core, precision=highest
            )
            image = jnp.einsum("lib,bm->lim", moved_own, next_sketch, precision=highest)
            image = image + jnp.einsum("lib,bm->lim", moved_other, other_sketch, precision=highest)
            gram_local = jnp.einsum("lim,lin->mn", image, image, precision=highest)
            cross_own = jnp.einsum("lim,lib->mb", image, moved_own, precision=highest)
            cross_other = jnp.einsum("lim,lib->mb", image, moved_other, precision=highest)
            return (moved_own, moved_other, image, gram_local, cross_own, cross_other)

        def spare_work():
            return (zero_block, zero_block, zero_block, zero_square, zero_square, zero_square)

        moved_own, moved_other, image, gram_local, cross_own, cross_other = lax.cond(
            active, heavy_work, spare_work
        )
        gram_local, cross_own, cross_other = lax.psum((gram_local, cross_own, cross_other), "split")
        shifted = gram_local + shift_ratio * jnp.trace(gram_local) / rank_dim * identity
        shifted = jnp.where(jnp.logical_and(active, jnp.logical_not(is_last)), shifted, identity)
        factor_low = jnp.linalg.cholesky(shifted)
        inverse = lax.linalg.triangular_solve(factor_low, identity, left_side=True, lower=True)
        ortho_core = lax.cond(
            active,
            lambda: jnp.einsum("lim,nm->lin", image, inverse, precision=highest),
            lambda: zero_block,
        )
        carry_own = jnp.dot(inverse, cross_own, precision=highest)
        carry_other = jnp.dot(inverse, cross_other, precision=highest)
        carry_new = jnp.concatenate([carry_own, carry_other], axis=1)
        out_piece = jnp.where(is_last, moved_own + moved_other, ortho_core) * out_scale
        result = jnp.where(active, out_piece, result)
        own_carry = jnp.where(active, carry_new, own_carry)
        return (own_carry, result)

    start_carry = jnp.zeros((rank_dim, 2 * rank_dim), jnp.float32)
    own_carry, result = lax.fori_loop(0, train_depth, carry_turn, (start_carry, zero_block))
    return result[None, None]


def solution(mesh):
    in_specs = (P("pair", "cores", None, "split", None), P("cores", None, "split", None))
    out_specs = P("pair", "cores", None, "split", None)
    return jax.shard_map(body, mesh=mesh, in_specs=in_specs, out_specs=out_specs, check_vma=False)
```

profile of v0, /device:TPU:27, one launch (start us, length us, event | category | flops | bytes accessed | tf_op | source)
XLA Modules:
  0.0 206.4 jit_solution(13391490821385702450)
XLA Ops:
  6.5 1.2 copy.23
  8.0 0.8 copy-done.4
  8.8 52.4 %while.36 = (s32[]{:T(128)}, f32[128,128]{1,0:T(8,128)S(1)}, f32[128,128]{1,0:T(8,128)S(1)}, s32[]{:T(128)}, pred[]{:T(512)}, /*index=5*/f32[128,8,128]{2,1,0:T(...) while((s32[]{:T(128)}, f32[128,128]{1,0:T(8,128)S(1)}, f32[128,128]{1,0:T(8,128)S(1)}, ...), condition=%wide.region_4.5_spmd.clone, body=%wide.region_0.4_spmd.clone.sunk | while | flops 402800640 | bytes 3735826 | solution.py:56
  8.8 2.6 %collective-permute-start = (f32[128,128]{1,0:T(8,128)S(1)}, f32[128,128]{1,0:T(8,128)S(1)}, u32[]{:S(2)}, u32[]{:S(2)}) collective-permute-start(f32[128,128]{1,0:T(8,128)S(1)} %broadcast_select_fusion.7), channel_id=1, source_target_pairs={{2,0},{3,1},{6,4},{7,5},{10,8},{11,9},{14,12},{15,13},{18,16},{19,... | collective-permute-start | bytes 196616 | tf_op jit(solution)/shard_map/while/body/eval_jaxpr/ppermute | solution.py:16
  11.4 0.9 collective-permute-done
  12.3 1.2 conditional.11
  12.3 0.6 fusion.4
  12.9 0.6 convolution_bitcast_fusion
  13.5 0.6 copy-done.9
  14.1 20.9 %all-reduce.6.cloned.1.call-done = f32[128,128]{1,0:T(8,128)} async-done(((f32[128,128]{1,0:T(8,128)}), f32[128,128]{1,0:T(8,128)}) %all-reduce.6.cloned.1.call-update) | async-done | bytes 65552 | tf_op jit(solution)/shard_map/while/body/eval_jaxpr/psum | solution.py:51
  35.1 0.9 broadcast_select_fusion.8
  36.0 2.2 %collective-permute-start = (f32[128,128]{1,0:T(8,128)S(1)}, f32[128,128]{1,0:T(8,128)S(1)}, u32[]{:S(2)}, u32[]{:S(2)}) collective-permute-start(f32[128,128]{1,0:T(8,128)S(1)} %broadcast_select_fusion.7), channel_id=1, source_target_pairs={{2,0},{3,1},{6,4},{7,5},{10,8},{11,9},{14,12},{15,13},{18,16},{19,... | collective-permute-start | bytes 196616 | tf_op jit(solution)/shard_map/while/body/eval_jaxpr/ppermute | solution.py:16
  38.2 0.9 collective-permute-done
  39.1 0.6 copy-done.9
  39.8 21.3 %all-reduce.6.cloned.1.call-done = f32[128,128]{1,0:T(8,128)} async-done(((f32[128,128]{1,0:T(8,128)}), f32[128,128]{1,0:T(8,128)}) %all-reduce.6.cloned.1.call-update) | async-done | bytes 65552 | tf_op jit(solution)/shard_map/while/body/eval_jaxpr/psum | solution.py:51
  61.5 0.7 pad_maximum_fusion
  62.2 4.0 %collective-permute-done.3 = f32[128,128]{1,0:T(8,128)S(1)} collective-permute-done((f32[128,128]{1,0:T(8,128)S(1)}, f32[128,128]{1,0:T(8,128)S(1)}, u32[]{:S(2)}, u32[]{:S(2)}) %collective-permute-start.3) | collective-permute-done | bytes 65568 | tf_op jit(solution)/shard_map/ppermute | solution.py:22
  66.1 132.6 %while.37 = (s32[]{:T(128)}, f32[128,256]{0,1:T(8,128)S(1)}, f32[128,8,128]{2,0,1:T(8,128)S(1)}, s32[]{:T(128)}, pred[]{:T(512)}, /*index=5*/pred[]{:T(512)}, f3...) while((s32[]{:T(128)}, f32[128,256]{0,1:T(8,128)S(1)}, ...), condition=%wide.region_16.17_spmd.clone.clone, body=%wide.region_5.16_spmd.clone.clone.sunk | while | flops 1687502976 | bytes 25757356 | solution.py:106
  66.1 1.3 collective-permute-start.1
  67.5 3.9 %collective-permute-done.1 = f32[128,256]{0,1:T(8,128)S(1)} collective-permute-done((f32[128,256]{0,1:T(8,128)S(1)}, f32[128,256]{0,1:T(8,128)S(1)}, u32[]{:S(2)}, u32[]{:S(2)}) %collective-permute-start.1) | collective-permute-done | bytes 131104 | tf_op jit(solution)/shard_map/while/body/eval_jaxpr/ppermute | solution.py:16
  71.3 0.9 conditional.12
  71.4 0.8 broadcast_in_dim.29.clone.1
  72.3 0.6 copy-done.6
  73.0 31.5 %all-reduce.8.cloned.1.call-done = (f32[128,128]{1,0:T(8,128)}, f32[128,128]{1,0:T(8,128)}, f32[128,128]{1,0:T(8,128)}) async-done(((f32[128,128]{1,0:T(8,128)}, f32[128,128]{1,0:T(8,128)}, f32[128,128]{1,0:T(8,128)}), (f32[128,128]{1,0:T(8,128)}, f32[128,128]{1,0:T(8,128)}, f32[128,128]{1,0:T(8,128)})) %all-reduce.8.cloned.1.call-update) | async-done | bytes 196624 | tf_op jit(solution)/shard_map/while/body/eval_jaxpr/psum | solution.py:87
  104.5 1.6 select_reduce_fusion.4
  106.9 11.7 %cholesky.87 = f32[128,128]{1,0:T(8,128)S(1)} custom-call(f32[128,128]{1,0:T(8,128)S(1)} %fusion.56), custom_call_target="Cholesky" | custom-call | tf_op jit(solution)/shard_map/while/body/eval_jaxpr/jit(cholesky)/cholesky | solution.py:90
  118.7 0.7 compare_reduce_fusion.2
  119.4 0.7 fusion.57
  120.1 9.8 %custom-call.27 = f32[1,128,128]{1,2,0:T(8,128)S(1)} custom-call(f32[1,128,128]{2,1,0:T(8,128)S(1)} %fusion.57), custom_call_target="InvertDiagBlocksLowerTriangular" | custom-call | tf_op jit(solution)/shard_map/while/body/eval_jaxpr/triangular_solve | solution.py:91
  132.3 1.3 collective-permute-start.1
  133.6 3.5 %collective-permute-done.1 = f32[128,256]{0,1:T(8,128)S(1)} collective-permute-done((f32[128,256]{0,1:T(8,128)S(1)}, f32[128,256]{0,1:T(8,128)S(1)}, u32[]{:S(2)}, u32[]{:S(2)}) %collective-permute-start.1) | collective-permute-done | bytes 131104 | tf_op jit(solution)/shard_map/while/body/eval_jaxpr/ppermute | solution.py:16
  137.2 9.7 %conditional.12 = (f32[128,8,128]{2,0,1:T(8,128)S(1)}, f32[128,8,128]{2,0,1:T(8,128)S(1)}, f32[128,8,128]{2,0,1:T(8,128)}, f32[128,128]{1,0:T(8,128)S(1)}, f32[1...) conditional(s32[]{:T(128)} %convert_element_type.70, () %tuple.117, (pred[]{:T(512)}, f32[128,256]{1,0:T(8,128)}, ...), branch_computations={%region_6.6_spmd, %region_7.7_spmd} | conditional | flops 1409449984 | bytes 16842912 | solution.py:84
  137.3 0.6 fusion.8
  138.5 0.6 fusion.7
  139.1 1.4 convolution_add_fusion
  140.4 2.0 convolution_bitcast_fusion.1
  142.5 2.0 convolution_bitcast_fusion.2
  144.5 2.3 %convolution_bitcast_fusion.3 = f32[128,128]{1,0:T(8,128)S(1)} fusion(f32[128,8,128]{2,0,1:T(8,128)} %convolution_add_fusion), kind=kOutput, calls=%fused_computation.9 | convolution fusion | flops 201326592 | bytes 589824 | tf_op jit(solution)/shard_map/while/body/eval_jaxpr/cond/branch_1_fun/lim,lin->mn/dot_general | solution.py:76
  146.9 0.6 copy-done.6
  147.6 21.8 %all-reduce.8.cloned.1.call-done = (f32[128,128]{1,0:T(8,128)}, f32[128,128]{1,0:T(8,128)}, f32[128,128]{1,0:T(8,128)}) async-done(((f32[128,128]{1,0:T(8,128)}, f32[128,128]{1,0:T(8,128)}, f32[128,128]{1,0:T(8,128)}), (f32[128,128]{1,0:T(8,128)}, f32[128,128]{1,0:T(8,128)}, f32[128,128]{1,0:T(8,128)})) %all-reduce.8.cloned.1.call-update) | async-done | bytes 196624 | tf_op jit(solution)/shard_map/while/body/eval_jaxpr/psum | solution.py:87
  169.4 1.6 select_reduce_fusion.4
  171.9 11.7 %cholesky.87 = f32[128,128]{1,0:T(8,128)S(1)} custom-call(f32[128,128]{1,0:T(8,128)S(1)} %fusion.56), custom_call_target="Cholesky" | custom-call | tf_op jit(solution)/shard_map/while/body/eval_jaxpr/jit(cholesky)/cholesky | solution.py:90
  183.6 0.7 compare_reduce_fusion.2
  184.3 0.7 fusion.57
  185.0 9.8 %custom-call.27 = f32[1,128,128]{1,2,0:T(8,128)S(1)} custom-call(f32[1,128,128]{2,1,0:T(8,128)S(1)} %fusion.57), custom_call_target="InvertDiagBlocksLowerTriangular" | custom-call | tf_op jit(solution)/shard_map/while/body/eval_jaxpr/triangular_solve | solution.py:91
  196.8 1.6 conditional.13
  196.8 1.6 fusion.12
  198.8 1.1 copy.22
  (89 shorter events, 6.7 us)
Async XLA Ops:
  6.5 1.4 copy-start.12
  7.7 1.0 copy-start.4
  7.7 58.4 %collective-permute-start.2 = (f32[128,8,128]{2,0,1:T(8,128)S(1)}, f32[128,8,128]{2,0,1:T(8,128)S(1)}, u32[]{:S(2)}, u32[]{:S(2)}) collective-permute-start(f32[128,8,128]{2,0,1:T(8,128)S(1)} %bitcast.77), channel_id=1, source_target_pairs={{0,24},{4,28},{8,0},{12,4},{16,8},{20,12},{24,16},{28,20},{1,25},{... | collective-permute-start | bytes 1572872 | tf_op jit(solution)/shard_map/ppermute | solution.py:22
  8.8 26.3 %all-reduce.6.cloned.1.call-start = ((), (), s32[]{:S(2)}) async-start(), calls=%async_computation | async-start | bytes 131072 | tf_op jit(solution)/shard_map/while/body/eval_jaxpr/psum | solution.py:51
  8.8 3.5 %collective-permute-start = (f32[128,128]{1,0:T(8,128)S(1)}, f32[128,128]{1,0:T(8,128)S(1)}, u32[]{:S(2)}, u32[]{:S(2)}) collective-permute-start(f32[128,128]{1,0:T(8,128)S(1)} %broadcast_select_fusion.7), channel_id=1, source_target_pairs={{2,0},{3,1},{6,4},{7,5},{10,8},{11,9},{14,12},{15,13},{18,16},{19,... | collective-permute-start | bytes 196616 | tf_op jit(solution)/shard_map/while/body/eval_jaxpr/ppermute | solution.py:16
  13.5 0.6 copy-start.9
  35.9 25.2 %all-reduce.6.cloned.1.call-start = ((), (), s32[]{:S(2)}) async-start(), calls=%async_computation | async-start | bytes 131072 | tf_op jit(solution)/shard_map/while/body/eval_jaxpr/psum | solution.py:51
  36.0 3.1 %collective-permute-start = (f32[128,128]{1,0:T(8,128)S(1)}, f32[128,128]{1,0:T(8,128)S(1)}, u32[]{:S(2)}, u32[]{:S(2)}) collective-permute-start(f32[128,128]{1,0:T(8,128)S(1)} %broadcast_select_fusion.7), channel_id=1, source_target_pairs={{2,0},{3,1},{6,4},{7,5},{10,8},{11,9},{14,12},{15,13},{18,16},{19,... | collective-permute-start | bytes 196616 | tf_op jit(solution)/shard_map/while/body/eval_jaxpr/ppermute | solution.py:16
  39.1 0.6 copy-start.9
  61.2 5.0 %collective-permute-start.3 = (f32[128,128]{1,0:T(8,128)S(1)}, f32[128,128]{1,0:T(8,128)S(1)}, u32[]{:S(2)}, u32[]{:S(2)}) collective-permute-start(f32[128,128]{1,0:T(8,128)S(1)} %get-tuple-element.843), channel_id=1, source_target_pairs={{0,24},{4,28},{8,0},{12,4},{16,8},{20,12},{24,16},{28,20},{1,25},{... | collective-permute-start | bytes 196616 | tf_op jit(solution)/shard_map/ppermute | solution.py:22
  66.1 38.3 %all-reduce.8.cloned.1.call-start = ((), (), s32[]{:S(2)}) async-start(), calls=%async_computation.1 | async-start | bytes 393216 | tf_op jit(solution)/shard_map/while/body/eval_jaxpr/psum | solution.py:87
  66.1 5.2 %collective-permute-start.1 = (f32[128,256]{0,1:T(8,128)S(1)}, f32[128,256]{0,1:T(8,128)S(1)}, u32[]{:S(2)}, u32[]{:S(2)}) collective-permute-start(f32[128,256]{0,1:T(8,128)S(1)} %broadcast_select_fusion.9), channel_id=1, source_target_pairs={{0,2},{1,3},{4,6},{5,7},{8,10},{9,11},{12,14},{13,15},{16,18},{17,... | collective-permute-start | bytes 393224 | tf_op jit(solution)/shard_map/while/body/eval_jaxpr/ppermute | solution.py:16
  72.3 0.6 copy-start.6
  72.3 0.6 copy-start.7
  72.3 0.7 copy-start.8
  104.5 2.3 %copy-start.5 = (f32[128,128]{1,0:T(8,128)S(1)}, f32[128,128]{1,0:T(8,128)}, u32[]{:S(2)}) copy-start(f32[128,128]{1,0:T(8,128)} %get-tuple-element.789) | copy-start | bytes 196612 | tf_op jit(solution)/shard_map/while
  129.9 0.8 copy-start.11
  130.7 0.8 copy-start.10
  132.2 37.2 %all-reduce.8.cloned.1.call-start = ((), (), s32[]{:S(2)}) async-start(), calls=%async_computation.1 | async-start | bytes 393216 | tf_op jit(solution)/shard_map/while/body/eval_jaxpr/psum | solution.py:87
  132.3 4.8 %collective-permute-start.1 = (f32[128,256]{0,1:T(8,128)S(1)}, f32[128,256]{0,1:T(8,128)S(1)}, u32[]{:S(2)}, u32[]{:S(2)}) collective-permute-start(f32[128,256]{0,1:T(8,128)S(1)} %broadcast_select_fusion.9), channel_id=1, source_target_pairs={{0,2},{1,3},{4,6},{5,7},{8,10},{9,11},{12,14},{13,15},{16,18},{17,... | collective-permute-start | bytes 393224 | tf_op jit(solution)/shard_map/while/body/eval_jaxpr/ppermute | solution.py:16
  137.9 4.6 %copy-start.2 = (f32[128,8,128]{2,0,1:T(8,128)}, f32[128,8,128]{2,0,1:T(8,128)S(1)}, u32[]{:S(2)}) copy-start(f32[128,8,128]{2,0,1:T(8,128)S(1)} %fusion.8) | copy-start | bytes 1572868 | tf_op jit(solution)/shard_map/while/body/eval_jaxpr/cond
  139.0 1.4 copy-start
  144.5 2.3 %copy-start.1 = (f32[128,8,128]{2,0,1:T(8,128)S(1)}, f32[128,8,128]{2,0,1:T(8,128)}, u32[]{:S(2)}) copy-start(f32[128,8,128]{2,0,1:T(8,128)} %copy-done) | copy-start | bytes 1572868 | tf_op jit(solution)/shard_map/while/body/eval_jaxpr/cond
  144.5 2.3 %copy-start.3 = (f32[128,8,128]{2,0,1:T(8,128)S(1)}, f32[128,8,128]{2,0,1:T(8,128)}, u32[]{:S(2)}) copy-start(f32[128,8,128]{2,0,1:T(8,128)} %copy-done.2) | copy-start | bytes 1572868 | tf_op jit(solution)/shard_map/while/body/eval_jaxpr/cond
  146.9 0.6 copy-start.6
  146.9 0.6 copy-start.7
  146.9 0.7 copy-start.8
  169.4 2.3 %copy-start.5 = (f32[128,128]{1,0:T(8,128)S(1)}, f32[128,128]{1,0:T(8,128)}, u32[]{:S(2)}) copy-start(f32[128,128]{1,0:T(8,128)} %get-tuple-element.789) | copy-start | bytes 196612 | tf_op jit(solution)/shard_map/while
  194.8 0.8 copy-start.11
  195.7 0.8 copy-start.10
Sparse Core Ops, SparseCore 0:
  14.2 20.7 all-reduce.5
  39.9 21.1 all-reduce.5
  73.1 31.2 all-reduce.7
  147.7 21.6 all-reduce.7
where the time goes:
time: 208 us; the launch traced here: 206 us
  waiting for transfers between devices  109 us (52%)
  other arithmetic  51.4 us (25%)
  matrix products  14 us (7%)
  between operations  13.1 us (6%)
  local copies, waits for them, and re-layouts  9.04 us (4%)
  starting transfers between devices  7.96 us (4%)
  loops' own time  2.13 us (1%)
    psum x2, waiting for transfers between devices, carry_turn(): lax.psum((gram_local, cross_own, cross_other), 'split')  53.3 us
    psum x2, waiting for transfers between devices, sketch_turn(): summed = lax.psum(partial_value, 'split')  42.3 us
    another operation x6, other arithmetic, carry_turn(): factor_low = jnp.linalg.cholesky(shifted)  24.9 us
    another operation x4, other arithmetic, carry_turn(): lax.linalg.triangular_solve(factor_low, identity, left_side=True, lower=T...  21 us
    ppermute x4, waiting for transfers between devices, passed_along(): return lax.ppermute(block, axis, route)  9.17 us
    ppermute x4, starting transfers between devices, passed_along(): return lax.ppermute(block, axis, route)  7.34 us
    while x28, local copies, waits for them, and re-layouts  4.73 us
  transfers between devices with their start and end apart: 10, of which 9 were waited for; matrix products, arithmetic and copies ran while one was open for 1% of the time, Pallas kernels for 0%

commit v1 on v0

v1 whole, which is shorter than its diff:
```python
import functools

import jax
import jax.numpy as jnp
from jax import lax
from jax.experimental import pallas as pl
from jax.experimental.pallas import tpu as pltpu
from jax.sharding import PartitionSpec as P

SHIFT_RATIO = 0.01
CHUNKS = 4
PANEL = 4
MESH = pl.DeviceIdType.MESH


def dot(a, b, dims=((1,), (0,))):
    return lax.dot_general(
        a, b, (dims, ((), ())), precision=lax.Precision.HIGHEST, preferred_element_type=jnp.float32
    )


def lower_inverse(shifted, inv_ref):
    n = shifted.shape[0]
    lane = lax.broadcasted_iota(jnp.int32, (1, n), 1)
    state = shifted
    top = 0
    for start in range(0, n, PANEL):
        inside = (lane >= start) & (lane < start + PANEL)
        cols, rows = [], []
        for j in range(start, start + PANEL):
            cols.append(jnp.broadcast_to(state[:, j : j + 1], state.shape))
            row = state[j - top : j - top + 1, :]
            rows.append(jnp.where(inside, jnp.where(lane == j, 1.0, 0.0), row))
        scaled = []
        for k in range(PANEL):
            at = start + k - top
            pivot = cols[k][at : at + 1, :]
            recip = 1.0 / pivot
            scaled.append(rows[k] * recip)
            for m in range(k + 1, PANEL):
                factor = cols[m][at : at + 1, :] * recip
                cols[m] = cols[m] - cols[k] * factor
                rows[m] = rows[m] - rows[k] * factor
            root = lax.rsqrt(pivot)
            root = root * (1.5 - 0.5 * pivot * root * root)
            inv_ref[start + k : start + k + 1, :] = jnp.where(lane <= start + k, rows[k] * root, 0.0)
        new_top = (start + PANEL) // 8 * 8
        if start + PANEL < n:
            drop = new_top - top
            update = jnp.where(inside, 0.0, state[drop:, :])
            for k in range(PANEL):
                update = update - cols[k][drop:, :] * scaled[k]
            state, top = update, new_top


def kernel(
    n_pair, depth, n_split, stride, scale,
    c_ref, sk_ref, out_ref,
    c_own, c_oth, sk32, y_buf, s_part, s_in, g_part, g_in, x_part, x_in, inv, carry_out, carry_in,
    local_sem, c_send, c_recv, s_send, s_recv, g_send, g_recv, x_send, x_recv, k_send, k_recv, go_sem,
):
    q = lax.axis_index("pair")
    p = lax.axis_index("cores")
    y = lax.axis_index("split")
    rank, modes, _ = c_own.shape
    last = depth - 1
    before = lax.rem(q - stride + n_pair, n_pair)
    after = lax.rem(q + stride, n_pair)

    def mate(d):
        return lax.rem(y + d + n_split, n_split)

    local = pltpu.make_async_copy(c_ref, c_own, local_sem)
    local.start()

    barrier = pltpu.get_barrier_semaphore()

    def greet(*place):
        pl.semaphore_signal(barrier, inc=1, device_id=place, device_id_type=MESH)

    greet(after, p, y)

    @pl.when(p < last)
    def _():
        for d in range(n_split):
            greet(q, p + 1, mate(d))
            greet(after, p + 1, mate(d))
        for d in range(1, n_split):
            greet(q, p, mate(-d))

    @pl.when(p > 0)
    def _():
        greet(q, p - 1, y)

    @pl.when(p == 0)
    def _():
        pl.semaphore_wait(barrier, 1 + (n_split - 1) + 1)

    if depth > 2:
        @pl.when((p > 0) & (p < last))
        def _():
            pl.semaphore_wait(barrier, 1 + (n_split - 1) + 1 + 2 * n_split)

    @pl.when(p == last)
    def _():
        pl.semaphore_wait(barrier, 1 + 2 * n_split)

    part = rank // CHUNKS

    def core_copy(k):
        rows = pl.ds(k * part, part)
        return pltpu.make_async_remote_copy(
            src_ref=c_ref.at[rows], dst_ref=c_oth.at[rows], send_sem=c_send.at[k], recv_sem=c_recv.at[k],
            device_id=(before, p, y), device_id_type=MESH,
        )

    def sketch_copy(which, d):
        return pltpu.make_async_remote_copy(
            src_ref=s_part, dst_ref=s_in.at[which, d],
            send_sem=s_send.at[which, d], recv_sem=s_recv.at[which, d],
            device_id=(q if which == 0 else before, p - 1, mate(d)), device_id_type=MESH,
        )

    def gram_copy(d):
        return pltpu.make_async_remote_copy(
            src_ref=g_part, dst_ref=g_in.at[d - 1], send_sem=g_send.at[d - 1], recv_sem=g_recv.at[d - 1],
            device_id=(q, p, mate(d)), device_id_type=MESH,
        )

    def cross_copy(d):
        return pltpu.make_async_remote_copy(
            src_ref=x_part, dst_ref=x_in.at[d - 1], send_sem=x_send.at[d - 1], recv_sem=x_recv.at[d - 1],
            device_id=(q, p, mate(d)), device_id_type=MESH,
        )

    def carry_copy():
        return pltpu.make_async_remote_copy(
            src_ref=carry_out, dst_ref=carry_in, send_sem=k_send, recv_sem=k_recv,
            device_id=(q, p + 1, y), device_id_type=MESH,
        )

    def send_core():
        for k in range(CHUNKS):
            core_copy(k).start()

    def receive_sketch():
        for which in range(2):
            for d in range(n_split):
                sketch_copy(which, d).wait_recv()
            total = s_in[which, 0]
            for d in range(1, n_split):
                total = total + s_in[which, d]
            s_in[which, 0] = total

    def send_sketch(at_end):
        sk32[...] = sk_ref[...].astype(jnp.float32)
        local.wait()
        if at_end:
            left = jnp.concatenate([c_own[:, i, :] for i in range(modes)], axis=1)
        else:
            inner = dot(c_own[...].reshape(rank * modes, rank), s_in[0, 0])
            y_buf[...] = inner.reshape(rank, modes, rank)
            left = jnp.concatenate([y_buf[:, i, :] for i in range(modes)], axis=1)
        right = jnp.concatenate([sk32[:, i, :] for i in range(modes)], axis=1)
        s_part[...] = dot(left, right, ((1,), (1,)))
        for which in (1, 0):
            for d in range(n_split):
                sketch_copy(which, d).start()

    def finish_sketch():
        for which in range(2):
            for d in range(n_split):
                sketch_copy(which, d).wait_send()

    def compress(waits):
        own_in, oth_in = s_in[0, 0], s_in[1, 0]
        gram = jnp.zeros((rank, rank), jnp.float32)
        for k in range(CHUNKS):
            rows = pl.ds(k * part, part)
            if waits:
                core_copy(k).wait_recv()
            own = c_own[rows].reshape(part * modes, rank)
            oth = c_oth[rows].reshape(part * modes, rank)
            image = dot(own, own_in) + dot(oth, oth_in)
            y_buf[rows] = image.reshape(part, modes, rank)
            gram = gram + dot(image, image, ((0,), (0,)))
        g_part[...] = gram
        for d in range(1, n_split):
            gram_copy(d).start()
        if waits:
            for k in range(CHUNKS):
                core_copy(k).wait_send()
            pl.semaphore_signal(go_sem, inc=1, device_id=(q, p + 1, y), device_id_type=MESH)
        flat = y_buf[...].reshape(rank * modes, rank)
        x_part[:, :rank] = dot(flat, c_own[...].reshape(rank * modes, rank), ((0,), (0,)))
        x_part[:, rank:] = dot(flat, c_oth[...].reshape(rank * modes, rank), ((0,), (0,)))
        for d in range(1, n_split):
            cross_copy(d).start()
        for d in range(1, n_split):
            gram_copy(d).wait_recv()
            gram = gram + g_in[d - 1]
        eye = (
            lax.broadcasted_iota(jnp.int32, (rank, rank), 0)
            == lax.broadcasted_iota(jnp.int32, (rank, rank), 1)
        )
        diagonal = jnp.where(eye, gram, 0.0)
        trace = jnp.sum(jnp.sum(diagonal, axis=0, keepdims=True), axis=1, keepdims=True)
        shifted = gram + jnp.where(eye, SHIFT_RATIO * trace / rank, 0.0)
        lower_inverse(shifted, inv)
        inverse = inv[...]
        cross = x_part[...]
        for d in range(1, n_split):
            cross_copy(d).wait_recv()
            cross = cross + x_in[d - 1]
        carry_out[...] = dot(inverse, cross)
        carry_copy().start()
        ortho = dot(flat, inverse * scale, ((1,), (1,)))
        out_ref[...] = ortho.reshape(rank, modes, rank)
        for d in range(1, n_split):
            gram_copy(d).wait_send()
            cross_copy(d).wait_send()
        carry_copy().wait_send()

    @pl.when(p == 0)
    def _():
        send_core()
        local.wait()
        receive_sketch()
        compress(True)

    if depth > 2:
        @pl.when((p > 0) & (p < last))
        def _():
            receive_sketch()
            send_sketch(False)
            pl.semaphore_wait(go_sem, 1)
            send_core()
            for k in range(CHUNKS):
                core_copy(k).wait_recv()
            for k in range(CHUNKS):
                core_copy(k).wait_send()
            pl.semaphore_signal(go_sem, inc=1, device_id=(q, p + 1, y), device_id_type=MESH)
            finish_sketch()
            carry_copy().wait_recv()
            for i in range(modes):
                c_own[:, i, :] = dot(carry_in[:, :rank], c_own[:, i, :])
                c_oth[:, i, :] = dot(carry_in[:, rank:], c_oth[:, i, :])
            compress(False)

    @pl.when(p == last)
    def _():
        send_sketch(True)
        pl.semaphore_wait(go_sem, 1)
        send_core()
        for k in range(CHUNKS):
            core_copy(k).wait_recv()
        top = jnp.concatenate([c_own[:, i, :] for i in range(modes)], axis=1)
        bottom = jnp.concatenate([c_oth[:, i, :] for i in range(modes)], axis=1)
        joined = jnp.concatenate([top, bottom], axis=0)
        finish_sketch()
        for k in range(CHUNKS):
            core_copy(k).wait_send()
        carry_copy().wait_recv()
        moved = dot(carry_in[...] * scale, joined)
        for i in range(modes):
            out_ref[:, i, :] = moved[:, i * rank : (i + 1) * rank]


def body(n_pair, depth, n_split, summand_cores, sketch_cores):
    own_core, sketch_core = summand_cores[0, 0], sketch_cores[0]
    rank, modes, _ = own_core.shape
    scale = (rank * modes * n_split) ** 0.5
    square, wide = (rank, rank), (rank, 2 * rank)
    others = n_split - 1
    vmem = lambda *shape: pltpu.VMEM(shape, jnp.float32)
    sems = lambda *shape: pltpu.SemaphoreType.DMA(shape)
    out = pl.pallas_call(
        functools.partial(kernel, n_pair, depth, n_split, n_pair // 4, scale),
        out_shape=jax.ShapeDtypeStruct(own_core.shape, jnp.float32),
        in_specs=[pl.BlockSpec(memory_space=pl.ANY), pl.BlockSpec(memory_space=pltpu.VMEM)],
        out_specs=pl.BlockSpec(memory_space=pltpu.VMEM),
        scratch_shapes=[
            vmem(*own_core.shape), vmem(*own_core.shape), vmem(*own_core.shape), vmem(*own_core.shape),
            vmem(*square), vmem(2, n_split, *square),
            vmem(*square), vmem(others, *square),
            vmem(*wide), vmem(others, *wide),
            vmem(*square), vmem(*wide), vmem(*wide),
            pltpu.SemaphoreType.DMA,
            sems(CHUNKS), sems(CHUNKS),
            sems(2, n_split), sems(2, n_split),
            sems(others), sems(others),
            sems(others), sems(others),
            pltpu.SemaphoreType.DMA, pltpu.SemaphoreType.DMA,
            pltpu.SemaphoreType.REGULAR,
        ],
        compiler_params=pltpu.CompilerParams(
            collective_id=0, has_side_effects=True, vmem_limit_bytes=32 * 1024 * 1024
        ),
    )(own_core, sketch_core)
    return out[None, None]


def solution(mesh):
    in_specs = (P("pair", "cores", None, "split", None), P("cores", None, "split", None))
    out_specs = P("pair", "cores", None, "split", None)
    inner = functools.partial(body, mesh.shape["pair"], mesh.shape["cores"], mesh.shape["split"])
    return jax.shard_map(inner, mesh=mesh, in_specs=in_specs, out_specs=out_specs, check_vma=False)
```

time: 208 us -> 28 us (0.13)
  waiting for transfers between devices: 109 us -> 0 us
  other arithmetic: 51.4 us -> 0 us
  Pallas kernels: 0 us -> 25 us
  matrix products: 14 us -> 0 us
  between operations: 13.1 us -> 0.01 us
  starting transfers between devices: 7.96 us -> 0 us
  local copies, waits for them, and re-layouts: 9.04 us -> 2.79 us
  loops' own time: 2.13 us -> 0 us
    psum x4 -> x0, waiting for transfers between devices: 95.5 us -> none  [the longest x2 53.3 us: carry_turn(): lax.psum((gram_local, cross_own, cross_other), 'split')]
    another operation x10 -> x0, other arithmetic: 45.9 us -> none  [the longest x6 24.9 us: carry_turn(): factor_low = jnp.linalg.cholesky(shifted)]
    pallas_call x0 -> x1, Pallas kernels: none -> 25 us  [body(): pl.pallas_call(functools.partial(kernel, n_pair, depth, n_split, n_pair /...]
    dot_general x14 -> x0, matrix products: 13.4 us -> none  [the longest x1 2.3 us: heavy_work(): gram_local = jnp.einsum('lim,lin->mn', image, image, precision=highest)]
    ppermute x6 -> x0, waiting for transfers between devices: 13.1 us -> none  [the longest x4 9.17 us: passed_along(): return lax.ppermute(block, axis, route)]
    ppermute x6 -> x0, starting transfers between devices: 7.87 us -> none  [the longest x4 7.34 us: passed_along(): return lax.ppermute(block, axis, route)]
    while x29 -> x0, local copies, waits for them, and re-layouts: 5.83 us -> none
    reduce_sum x2 -> x0, other arithmetic: 3.23 us -> none  [carry_turn(): jnp.trace(gram_local)]
  transfers between devices with their start and end apart: 10 -> 0, of which waited for: 9 -> 0; matrix products, arithmetic and copies ran while one was open for 1% -> 0% of each run, Pallas kernels for 0% -> 0%
where the time goes in v1:
time: 28 us; the launch traced here: 27.8 us
  Pallas kernels  25 us (89%)
  local copies, waits for them, and re-layouts  2.79 us (10%)
    pallas_call x1, Pallas kernels, body(): pl.pallas_call(functools.partial(kernel, n_pair, depth, n_split, n_pair /...  25 us
    unnamed x5, local copies, waits for them, and re-layouts  2.79 us

profile of v1, /device:TPU:27, one launch (start us, length us, event | category | flops | bytes accessed | tf_op | source)
XLA Modules:
  0.0 27.8 jit_solution(9422205079555948672)
XLA Ops:
  0.0 0.0 copy-start
  0.0 1.0 %copy-done = f32[1,1,128,8,128]{4,3,2,1,0:T(8,128)S(1)} copy-done((f32[1,1,128,8,128]{4,3,2,1,0:T(8,128)S(1)}, f32[1,1,128,8,128]{4,3,2,1,0:T(8,128)}, u32[]{:S(2)}) %copy-start) | copy-done | bytes 524312
  1.0 0.0 copy-start.1
  1.0 0.9 %copy-done.1 = bf16[1,128,8,128]{3,2,1,0:T(8,128)(2,1)S(1)} copy-done((bf16[1,128,8,128]{3,2,1,0:T(8,128)(2,1)S(1)}, bf16[1,128,8,128]{3,2,1,0:T(8,128)(2,1)}, u32[]{:S(2)}) %copy-start.1) | copy-done | bytes 262168
  2.0 25.0 %shard_map.28 = f32[128,8,128]{2,1,0:T(8,128)S(1)} custom-call(f32[128,8,128]{2,1,0:T(8,128)S(1)} %bitcast.4, bf16[128,8,128]{2,1,0:T(8,128)(2,1)S(1)} %bitcast.5), custom_call_target="tpu_custom_call" | custom-call | tf_op jit(solution)/shard_map/pallas_call | solution.py:277
  27.0 0.8 %copy.4 = f32[1,1,128,8,128]{4,3,2,1,0:T(8,128)} copy(f32[1,1,128,8,128]{4,3,2,1,0:T(8,128)S(1)} %bitcast.3) | data formatting | bytes 1048576
Async XLA Ops:
  0.0 1.0 %copy-start = (f32[1,1,128,8,128]{4,3,2,1,0:T(8,128)S(1)}, f32[1,1,128,8,128]{4,3,2,1,0:T(8,128)}, u32[]{:S(2)}) copy-start(f32[1,1,128,8,128]{4,3,2,1,0:T(8,128)} %param.2) | copy-start | bytes 1572868
  1.0 0.9 %copy-start.1 = (bf16[1,128,8,128]{3,2,1,0:T(8,128)(2,1)S(1)}, bf16[1,128,8,128]{3,2,1,0:T(8,128)(2,1)}, u32[]{:S(2)}) copy-start(bf16[1,128,8,128]{3,2,1,0:T(8,128)(2,1)} %param.3) | copy-start | bytes 786436

commit v2 on v1

--- a/solution.py
+++ b/solution.py
@@ -8,8 +8,8 @@
 from jax.sharding import PartitionSpec as P
 
 SHIFT_RATIO = 0.01
-CHUNKS = 4
-PANEL = 4
+CHUNKS = 8
+PANEL = 8
 MESH = pl.DeviceIdType.MESH
 
 
@@ -56,8 +56,8 @@
 def kernel(
     n_pair, depth, n_split, stride, scale,
     c_ref, sk_ref, out_ref,
-    c_own, c_oth, sk32, y_buf, s_part, s_in, g_part, g_in, x_part, x_in, inv, carry_out, carry_in,
-    local_sem, c_send, c_recv, s_send, s_recv, g_send, g_recv, x_send, x_recv, k_send, k_recv, go_sem,
+    c_own, c_oth, sk16, sk32, y_buf, s_part, s_in, g_part, g_in, g_prev, x_part, x_prev, inv,
+    local_sem, local_sk_sem, c_send, c_recv, s_send, s_recv, g_send, g_recv, h_send, h_recv, x_send, x_recv, go_sem,
 ):
     q = lax.axis_index("pair")
     p = lax.axis_index("cores")
@@ -72,6 +72,8 @@
 
     local = pltpu.make_async_copy(c_ref, c_own, local_sem)
     local.start()
+    local_sk = pltpu.make_async_copy(sk_ref, sk16, local_sk_sem)
+    local_sk.start()
 
     barrier = pltpu.get_barrier_semaphore()
 
@@ -90,16 +92,17 @@
 
     @pl.when(p > 0)
     def _():
-        greet(q, p - 1, y)
+        for d in range(n_split):
+            greet(q, p - 1, mate(-d))
 
     @pl.when(p == 0)
     def _():
-        pl.semaphore_wait(barrier, 1 + (n_split - 1) + 1)
+        pl.semaphore_wait(barrier, 1 + (n_split - 1) + n_split)
 
     if depth > 2:
         @pl.when((p > 0) & (p < last))
         def _():
-            pl.semaphore_wait(barrier, 1 + (n_split - 1) + 1 + 2 * n_split)
+            pl.semaphore_wait(barrier, 1 + (n_split - 1) + 3 * n_split)
 
     @pl.when(p == last)
     def _():
@@ -127,33 +130,33 @@
             device_id=(q, p, mate(d)), device_id_type=MESH,
         )
 
+    def gram_on_copy(d):
+        return pltpu.make_async_remote_copy(
+            src_ref=g_part, dst_ref=g_prev.at[d], send_sem=h_send.at[d], recv_sem=h_recv.at[d],
+            device_id=(q, p + 1, mate(d)), device_id_type=MESH,
+        )
+
     def cross_copy(d):
         return pltpu.make_async_remote_copy(
-            src_ref=x_part, dst_ref=x_in.at[d - 1], send_sem=x_send.at[d - 1], recv_sem=x_recv.at[d - 1],
-            device_id=(q, p, mate(d)), device_id_type=MESH,
-        )
-
-    def carry_copy():
-        return pltpu.make_async_remote_copy(
-            src_ref=carry_out, dst_ref=carry_in, send_sem=k_send, recv_sem=k_recv,
-            device_id=(q, p + 1, y), device_id_type=MESH,
+            src_ref=x_part, dst_ref=x_prev.at[d], send_sem=x_send.at[d], recv_sem=x_recv.at[d],
+            device_id=(q, p + 1, mate(d)), device_id_type=MESH,
         )
 
     def send_core():
         for k in range(CHUNKS):
             core_copy(k).start()
 
-    def receive_sketch():
-        for which in range(2):
-            for d in range(n_split):
-                sketch_copy(which, d).wait_recv()
-            total = s_in[which, 0]
-            for d in range(1, n_split):
-                total = total + s_in[which, d]
-            s_in[which, 0] = total
+    def receive_sketch(which):
+        for d in range(n_split):
+            sketch_copy(which, d).wait_recv()
+        total = s_in[which, 0]
+        for d in range(1, n_split):
+            total = total + s_in[which, d]
+        s_in[which, 0] = total
 
     def send_sketch(at_end):
-        sk32[...] = sk_ref[...].astype(jnp.float32)
+        local_sk.wait()
+        sk32[...] = sk16[...].astype(jnp.float32)
         local.wait()
         if at_end:
             left = jnp.concatenate([c_own[:, i, :] for i in range(modes)], axis=1)
@@ -172,66 +175,91 @@
             for d in range(n_split):
                 sketch_copy(which, d).wait_send()
 
-    def compress(waits):
-        own_in, oth_in = s_in[0, 0], s_in[1, 0]
+    def pass_turn():
+        pl.semaphore_signal(go_sem, inc=1, device_id=(q, p + 1, y), device_id_type=MESH)
+
+    def factor(gram):
+        eye = (
+            lax.broadcasted_iota(jnp.int32, (rank, rank), 0)
+            == lax.broadcasted_iota(jnp.int32, (rank, rank), 1)
+        )
+        diagonal = jnp.where(eye, gram, 0.0)
+        trace = jnp.sum(jnp.sum(diagonal, axis=0, keepdims=True), axis=1, keepdims=True)
+        lower_inverse(gram + jnp.where(eye, SHIFT_RATIO * trace / rank, 0.0), inv)
+        return inv[...]
+
+    def carry_of_previous():
+        for d in range(n_split):
+            gram_on_copy(d).wait_recv()
+        gram = g_prev[0]
+        for d in range(1, n_split):
+            gram = gram + g_prev[d]
+        inverse = factor(gram)
+        for d in range(n_split):
+            cross_copy(d).wait_recv()
+        cross = x_prev[0]
+        for d in range(1, n_split):
+            cross = cross + x_prev[d]
+        return dot(inverse, cross)
+
+    def compress(first):
+        flat = (rank * modes, rank)
+        if first:
+            receive_sketch(0)
+        y_buf[...] = dot(c_own[...].reshape(flat), s_in[0, 0]).reshape(c_own.shape)
+        if first:
+            receive_sketch(1)
+        oth_in = s_in[1, 0]
         gram = jnp.zeros((rank, rank), jnp.float32)
         for k in range(CHUNKS):
             rows = pl.ds(k * part, part)
-            if waits:
+            if first:
+                if k == CHUNKS - 1:
+                    for m in range(CHUNKS - 1):
+                        core_copy(m).wait_send()
+                    pass_turn()
                 core_copy(k).wait_recv()
-            own = c_own[rows].reshape(part * modes, rank)
             oth = c_oth[rows].reshape(part * modes, rank)
-            image = dot(own, own_in) + dot(oth, oth_in)
+            image = y_buf[rows].reshape(part * modes, rank) + dot(oth, oth_in)
             y_buf[rows] = image.reshape(part, modes, rank)
             gram = gram + dot(image, image, ((0,), (0,)))
         g_part[...] = gram
         for d in range(1, n_split):
             gram_copy(d).start()
-        if waits:
-            for k in range(CHUNKS):
-                core_copy(k).wait_send()
-            pl.semaphore_signal(go_sem, inc=1, device_id=(q, p + 1, y), device_id_type=MESH)
-        flat = y_buf[...].reshape(rank * modes, rank)
-        x_part[:, :rank] = dot(flat, c_own[...].reshape(rank * modes, rank), ((0,), (0,)))
-        x_part[:, rank:] = dot(flat, c_oth[...].reshape(rank * modes, rank), ((0,), (0,)))
-        for d in range(1, n_split):
+        for d in range(n_split):
+            gram_on_copy(d).start()
+        if first:
+            core_copy(CHUNKS - 1).wait_send()
+        image = y_buf[...].reshape(flat)
+        x_part[:, :rank] = dot(image, c_own[...].reshape(flat), ((0,), (0,)))
+        x_part[:, rank:] = dot(image, c_oth[...].reshape(flat), ((0,), (0,)))
+        for d in range(n_split):
             cross_copy(d).start()
+        total = gram
         for d in range(1, n_split):
             gram_copy(d).wait_recv()
-            gram = gram + g_in[d - 1]
-        eye = (
-            lax.broadcasted_iota(jnp.int32, (rank, rank), 0)
-            == lax.broadcasted_iota(jnp.int32, (rank, rank), 1)
-        )
-        diagonal = jnp.where(eye, gram, 0.0)
-        trace = jnp.sum(jnp.sum(diagonal, axis=0, keepdims=True), axis=1, keepdims=True)
-        shifted = gram + jnp.where(eye, SHIFT_RATIO * trace / rank, 0.0)
-        lower_inverse(shifted, inv)
-        inverse = inv[...]
-        cross = x_part[...]
-        for d in range(1, n_split):
-            cross_copy(d).wait_recv()
-            cross = cross + x_in[d - 1]
-        carry_out[...] = dot(inverse, cross)
-        carry_copy().start()
-        ortho = dot(flat, inverse * scale, ((1,), (1,)))
+            total = total + g_in[d - 1]
+        inverse = factor(total)
+        ortho = dot(image, inverse * scale, ((1,), (1,)))
         out_ref[...] = ortho.reshape(rank, modes, rank)
         for d in range(1, n_split):
             gram_copy(d).wait_send()
+        for d in range(n_split):
+            gram_on_copy(d).wait_send()
             cross_copy(d).wait_send()
-        carry_copy().wait_send()
 
     @pl.when(p == 0)
     def _():
         send_core()
+        local_sk.wait()
         local.wait()
-        receive_sketch()
         compress(True)
 
     if depth > 2:
         @pl.when((p > 0) & (p < last))
         def _():
-            receive_sketch()
+            receive_sketch(0)
+            receive_sketch(1)
             send_sketch(False)
             pl.semaphore_wait(go_sem, 1)
             send_core()
@@ -239,12 +267,12 @@
                 core_copy(k).wait_recv()
             for k in range(CHUNKS):
                 core_copy(k).wait_send()
-            pl.semaphore_signal(go_sem, inc=1, device_id=(q, p + 1, y), device_id_type=MESH)
+            pass_turn()
             finish_sketch()
-            carry_copy().wait_recv()
+            carry = carry_of_previous()
             for i in range(modes):
-                c_own[:, i, :] = dot(carry_in[:, :rank], c_own[:, i, :])
-                c_oth[:, i, :] = dot(carry_in[:, rank:], c_oth[:, i, :])
+                c_own[:, i, :] = dot(carry[:, :rank], c_own[:, i, :])
+                c_oth[:, i, :] = dot(carry[:, rank:], c_oth[:, i, :])
             compress(False)
 
     @pl.when(p == last)
@@ -252,18 +280,18 @@
         send_sketch(True)
         pl.semaphore_wait(go_sem, 1)
         send_core()
+        carry = carry_of_previous() * scale
+        finish_sketch()
+        top = jnp.concatenate([c_own[:, i, :] for i in range(modes)], axis=1)
+        moved = dot(carry[:, :rank], top)
         for k in range(CHUNKS):
             core_copy(k).wait_recv()
-        top = jnp.concatenate([c_own[:, i, :] for i in range(modes)], axis=1)
         bottom = jnp.concatenate([c_oth[:, i, :] for i in range(modes)], axis=1)
-        joined = jnp.concatenate([top, bottom], axis=0)
-        finish_sketch()
+        moved = moved + dot(carry[:, rank:], bottom)
+        for i in range(modes):
+            out_ref[:, i, :] = moved[:, i * rank : (i + 1) * rank]
         for k in range(CHUNKS):
             core_copy(k).wait_send()
-        carry_copy().wait_recv()
-        moved = dot(carry_in[...] * scale, joined)
-        for i in range(modes):
-            out_ref[:, i, :] = moved[:, i * rank : (i + 1) * rank]
 
 
 def body(n_pair, depth, n_split, summand_cores, sketch_cores):
@@ -277,24 +305,25 @@
     out = pl.pallas_call(
         functools.partial(kernel, n_pair, depth, n_split, n_pair // 4, scale),
         out_shape=jax.ShapeDtypeStruct(own_core.shape, jnp.float32),
-        in_specs=[pl.BlockSpec(memory_space=pl.ANY), pl.BlockSpec(memory_space=pltpu.VMEM)],
+        in_specs=[pl.BlockSpec(memory_space=pltpu.HBM)] * 2,
         out_specs=pl.BlockSpec(memory_space=pltpu.VMEM),
         scratch_shapes=[
-            vmem(*own_core.shape), vmem(*own_core.shape), vmem(*own_core.shape), vmem(*own_core.shape),
+            vmem(*own_core.shape), vmem(*own_core.shape),
+            pltpu.VMEM(sketch_core.shape, sketch_core.dtype), vmem(*sketch_core.shape), vmem(*own_core.shape),
             vmem(*square), vmem(2, n_split, *square),
-            vmem(*square), vmem(others, *square),
-            vmem(*wide), vmem(others, *wide),
-            vmem(*square), vmem(*wide), vmem(*wide),
-            pltpu.SemaphoreType.DMA,
+            vmem(*square), vmem(others, *square), vmem(n_split, *square),
+            vmem(*wide), vmem(n_split, *wide),
+            vmem(*square),
+            pltpu.SemaphoreType.DMA, pltpu.SemaphoreType.DMA,
             sems(CHUNKS), sems(CHUNKS),
             sems(2, n_split), sems(2, n_split),
             sems(others), sems(others),
-            sems(others), sems(others),
-            pltpu.SemaphoreType.DMA, pltpu.SemaphoreType.DMA,
+            sems(n_split), sems(n_split),
+            sems(n_split), sems(n_split),
             pltpu.SemaphoreType.REGULAR,
         ],
         compiler_params=pltpu.CompilerParams(
-            collective_id=0, has_side_effects=True, vmem_limit_bytes=32 * 1024 * 1024
+            collective_id=0, has_side_effects=True, vmem_limit_bytes=65000 * 1024
         ),
     )(own_core, sketch_core)
     return out[None, None]

time: 28 us -> 26.8 us (0.957)
  local copies, waits for them, and re-layouts: 2.79 us -> 1.87 us
    unnamed x5 -> x1, local copies, waits for them, and re-layouts: 2.79 us -> 1.87 us
where the time goes in v2:
time: 26.8 us; the launch traced here: 26.7 us
  Pallas kernels  24.8 us (93%)
  local copies, waits for them, and re-layouts  1.87 us (7%)
    pallas_call x1, Pallas kernels, body(): pl.pallas_call(functools.partial(kernel, n_pair, depth, n_split, n_pair /...  24.8 us
    unnamed x1, local copies, waits for them, and re-layouts  1.87 us

profile of v2, /device:TPU:27, one launch (start us, length us, event | category | flops | bytes accessed | tf_op | source)
XLA Modules:
  0.0 26.7 jit_solution(16350353146920446044)
XLA Ops:
  0.0 24.8 %shard_map.28 = f32[128,8,128]{2,1,0:T(8,128)} custom-call(f32[128,8,128]{2,1,0:T(8,128)} %bitcast.4, bf16[128,8,128]{2,1,0:T(8,128)(2,1)} %bitcast.5), custom_call_target="tpu_custom_call" | custom-call | tf_op jit(solution)/shard_map/pallas_call | solution.py:305
  24.8 1.9 %copy.4 = f32[1,1,128,8,128]{4,3,2,1,0:T(8,128)} copy(f32[1,1,128,8,128]{4,3,2,1,0:T(8,128)} %bitcast.3) | data formatting | bytes 1048576

commit v3 on v2

--- a/solution.py
+++ b/solution.py
@@ -8,7 +8,7 @@
 from jax.sharding import PartitionSpec as P
 
 SHIFT_RATIO = 0.01
-CHUNKS = 8
+CHUNKS = 4
 PANEL = 8
 MESH = pl.DeviceIdType.MESH
 
@@ -17,6 +17,18 @@
     return lax.dot_general(
         a, b, (dims, ((), ())), precision=lax.Precision.HIGHEST, preferred_element_type=jnp.float32
     )
+
+
+def dot_exact_right(a, b):
+    total = None
+    for _ in range(3):
+        term = a.astype(jnp.bfloat16)
+        a = a - term.astype(jnp.float32)
+        piece = lax.dot_general(
+            term, b, (((1,), (1,)), ((), ())), preferred_element_type=jnp.float32
+        )
+        total = piece if total is None else total + piece
+    return total
 
 
 def lower_inverse(shifted, inv_ref):
@@ -165,7 +177,7 @@
             y_buf[...] = inner.reshape(rank, modes, rank)
             left = jnp.concatenate([y_buf[:, i, :] for i in range(modes)], axis=1)
         right = jnp.concatenate([sk32[:, i, :] for i in range(modes)], axis=1)
-        s_part[...] = dot(left, right, ((1,), (1,)))
+        s_part[...] = dot_exact_right(left, right.astype(jnp.bfloat16))
         for which in (1, 0):
             for d in range(n_split):
                 sketch_copy(which, d).start()
@@ -203,45 +215,54 @@
         return dot(inverse, cross)
 
     def compress(first):
-        flat = (rank * modes, rank)
         if first:
             receive_sketch(0)
-        y_buf[...] = dot(c_own[...].reshape(flat), s_in[0, 0]).reshape(c_own.shape)
-        if first:
             receive_sketch(1)
-        oth_in = s_in[1, 0]
-        gram = jnp.zeros((rank, rank), jnp.float32)
-        for k in range(CHUNKS):
+        g_part[...] = jnp.zeros(g_part.shape, jnp.float32)
+        x_part[...] = jnp.zeros(x_part.shape, jnp.float32)
+
+        def chunk_turn(k, _):
             rows = pl.ds(k * part, part)
             if first:
-                if k == CHUNKS - 1:
+                @pl.when(k == CHUNKS - 1)
+                def _():
                     for m in range(CHUNKS - 1):
                         core_copy(m).wait_send()
                     pass_turn()
+
                 core_copy(k).wait_recv()
+            own = c_own[rows].reshape(part * modes, rank)
             oth = c_oth[rows].reshape(part * modes, rank)
-            image = y_buf[rows].reshape(part * modes, rank) + dot(oth, oth_in)
+            image = dot(own, s_in[0, 0]) + dot(oth, s_in[1, 0])
             y_buf[rows] = image.reshape(part, modes, rank)
-            gram = gram + dot(image, image, ((0,), (0,)))
-        g_part[...] = gram
+            flipped = image.T
+            g_part[...] += dot(flipped, image)
+            x_part[:, :rank] += dot(flipped, own)
+            x_part[:, rank:] += dot(flipped, oth)
+            return 0
+
+        lax.fori_loop(0, CHUNKS, chunk_turn, 0)
         for d in range(1, n_split):
             gram_copy(d).start()
         for d in range(n_split):
             gram_on_copy(d).start()
+        for d in range(n_split):
+            cross_copy(d).start()
         if first:
             core_copy(CHUNKS - 1).wait_send()
-        image = y_buf[...].reshape(flat)
-        x_part[:, :rank] = dot(image, c_own[...].reshape(flat), ((0,), (0,)))
-        x_part[:, rank:] = dot(image, c_oth[...].reshape(flat), ((0,), (0,)))
-        for d in range(n_split):
-            cross_copy(d).start()
-        total = gram
+        total = g_part[...]
         for d in range(1, n_split):
             gram_copy(d).wait_recv()
             total = total + g_in[d - 1]
-        inverse = factor(total)
-        ortho = dot(image, inverse * scale, ((1,), (1,)))
-        out_ref[...] = ortho.reshape(rank, modes, rank)
+        inverse = (factor(total) * scale).T
+
+        def ortho_turn(k, _):
+            rows = pl.ds(k * part, part)
+            image = y_buf[rows].reshape(part * modes, rank)
+            out_ref[rows] = dot(image, inverse).reshape(part, modes, rank)
+            return 0
+
+        lax.fori_loop(0, CHUNKS, ortho_turn, 0)
         for d in range(1, n_split):
             gram_copy(d).wait_send()
         for d in range(n_split):

time: 26.8 us -> 28.1 us (1.049)
  Pallas kernels: 24.8 us -> 26 us
    pallas_call x1, Pallas kernels: 24.8 us -> 26 us  [body(): pl.pallas_call(functools.partial(kernel, n_pair, depth, n_split, n_pair /...]
where the time goes in v3:
time: 28.1 us; the launch traced here: 27.9 us
  Pallas kernels  26 us (93%)
  local copies, waits for them, and re-layouts  1.87 us (7%)
    pallas_call x1, Pallas kernels, body(): pl.pallas_call(functools.partial(kernel, n_pair, depth, n_split, n_pair /...  26 us
    unnamed x1, local copies, waits for them, and re-layouts  1.87 us

profile of v3, /device:TPU:27, one launch (start us, length us, event | category | flops | bytes accessed | tf_op | source)
XLA Modules:
  0.0 27.9 jit_solution(2896029476148944472)
XLA Ops:
  0.0 26.0 %shard_map.28 = f32[128,8,128]{2,1,0:T(8,128)} custom-call(f32[128,8,128]{2,1,0:T(8,128)} %bitcast.4, bf16[128,8,128]{2,1,0:T(8,128)(2,1)} %bitcast.5), custom_call_target="tpu_custom_call" | custom-call | tf_op jit(solution)/shard_map/pallas_call | solution.py:326
  26.1 1.9 %copy.4 = f32[1,1,128,8,128]{4,3,2,1,0:T(8,128)} copy(f32[1,1,128,8,128]{4,3,2,1,0:T(8,128)} %bitcast.3) | data formatting | bytes 1048576

commit v4 on v2

--- a/solution.py
+++ b/solution.py
@@ -17,6 +17,18 @@
     return lax.dot_general(
         a, b, (dims, ((), ())), precision=lax.Precision.HIGHEST, preferred_element_type=jnp.float32
     )
+
+
+def dot_exact_right(a, b):
+    total = None
+    for _ in range(3):
+        term = a.astype(jnp.bfloat16)
+        a = a - term.astype(jnp.float32)
+        piece = lax.dot_general(
+            term, b, (((1,), (1,)), ((), ())), preferred_element_type=jnp.float32
+        )
+        total = piece if total is None else total + piece
+    return total
 
 
 def lower_inverse(shifted, inv_ref):
@@ -54,7 +66,7 @@
 
 
 def kernel(
-    n_pair, depth, n_split, stride, scale,
+    n_pair, depth, n_split, stride,
     c_ref, sk_ref, out_ref,
     c_own, c_oth, sk16, sk32, y_buf, s_part, s_in, g_part, g_in, g_prev, x_part, x_prev, inv,
     local_sem, local_sk_sem, c_send, c_recv, s_send, s_recv, g_send, g_recv, h_send, h_recv, x_send, x_recv, go_sem,
@@ -95,66 +107,7 @@
         for d in range(n_split):
             greet(q, p - 1, mate(-d))
 
-    @pl.when(p == 0)
-    def _():
-        pl.semaphore_wait(barrier, 1 + (n_split - 1) + n_split)
-
-    if depth > 2:
-        @pl.when((p > 0) & (p < last))
-        def _():
-            pl.semaphore_wait(barrier, 1 + (n_split - 1) + 3 * n_split)
-
-    @pl.when(p == last)
-    def _():
-        pl.semaphore_wait(barrier, 1 + 2 * n_split)
-
-    part = rank // CHUNKS
-
-    def core_copy(k):
-        rows = pl.ds(k * part, part)
-        return pltpu.make_async_remote_copy(
-            src_ref=c_ref.at[rows], dst_ref=c_oth.at[rows], send_sem=c_send.at[k], recv_sem=c_recv.at[k],
-            device_id=(before, p, y), device_id_type=MESH,
-        )
-
-    def sketch_copy(which, d):
-        return pltpu.make_async_remote_copy(
-            src_ref=s_part, dst_ref=s_in.at[which, d],
-            send_sem=s_send.at[which, d], recv_sem=s_recv.at[which, d],
-            device_id=(q if which == 0 else before, p - 1, mate(d)), device_id_type=MESH,
-        )
-
-    def gram_copy(d):
-        return pltpu.make_async_remote_copy(
-            src_ref=g_part, dst_ref=g_in.at[d - 1], send_sem=g_send.at[d - 1], recv_sem=g_recv.at[d - 1],
-            device_id=(q, p, mate(d)), device_id_type=MESH,
-        )
-
-    def gram_on_copy(d):
-        return pltpu.make_async_remote_copy(
-            src_ref=g_part, dst_ref=g_prev.at[d], send_sem=h_send.at[d], recv_sem=h_recv.at[d],
-            device_id=(q, p + 1, mate(d)), device_id_type=MESH,
-        )
-
-    def cross_copy(d):
-        return pltpu.make_async_remote_copy(
-            src_ref=x_part, dst_ref=x_prev.at[d], send_sem=x_send.at[d], recv_sem=x_recv.at[d],
-            device_id=(q, p + 1, mate(d)), device_id_type=MESH,
-        )
-
-    def send_core():
-        for k in range(CHUNKS):
-            core_copy(k).start()
-
-    def receive_sketch(which):
-        for d in range(n_split):
-            sketch_copy(which, d).wait_recv()
-        total = s_in[which, 0]
-        for d in range(1, n_split):
-            total = total + s_in[which, d]
-        s_in[which, 0] = total
-
-    def send_sketch(at_end):
+    def make_sketch(at_end):
         local_sk.wait()
         sk32[...] = sk16[...].astype(jnp.float32)
         local.wait()
@@ -165,7 +118,72 @@
             y_buf[...] = inner.reshape(rank, modes, rank)
             left = jnp.concatenate([y_buf[:, i, :] for i in range(modes)], axis=1)
         right = jnp.concatenate([sk32[:, i, :] for i in range(modes)], axis=1)
-        s_part[...] = dot(left, right, ((1,), (1,)))
+        s_part[...] = dot_exact_right(left, right.astype(jnp.bfloat16))
+
+    @pl.when(p == last)
+    def _():
+        make_sketch(True)
+
+    @pl.when(p == 0)
+    def _():
+        pl.semaphore_wait(barrier, 1 + (n_split - 1) + n_split)
+
+    if depth > 2:
+        @pl.when((p > 0) & (p < last))
+        def _():
+            pl.semaphore_wait(barrier, 1 + (n_split - 1) + 3 * n_split)
+
+    @pl.when(p == last)
+    def _():
+        pl.semaphore_wait(barrier, 1 + 2 * n_split)
+
+    part = rank // CHUNKS
+
+    def core_copy(k):
+        rows = pl.ds(k * part, part)
+        return pltpu.make_async_remote_copy(
+            src_ref=c_ref.at[rows], dst_ref=c_oth.at[rows], send_sem=c_send.at[k], recv_sem=c_recv.at[k],
+            device_id=(before, p, y), device_id_type=MESH,
+        )
+
+    def sketch_copy(which, d):
+        return pltpu.make_async_remote_copy(
+            src_ref=s_part, dst_ref=s_in.at[which, d],
+            send_sem=s_send.at[which, d], recv_sem=s_recv.at[which, d],
+            device_id=(q if which == 0 else before, p - 1, mate(d)), device_id_type=MESH,
+        )
+
+    def gram_copy(d):
+        return pltpu.make_async_remote_copy(
+            src_ref=g_part, dst_ref=g_in.at[d - 1], send_sem=g_send.at[d - 1], recv_sem=g_recv.at[d - 1],
+            device_id=(q, p, mate(d)), device_id_type=MESH,
+        )
+
+    def gram_on_copy(d):
+        return pltpu.make_async_remote_copy(
+            src_ref=g_part, dst_ref=g_prev.at[d], send_sem=h_send.at[d], recv_sem=h_recv.at[d],
+            device_id=(q, p + 1, mate(d)), device_id_type=MESH,
+        )
+
+    def cross_copy(d):
+        return pltpu.make_async_remote_copy(
+            src_ref=x_part, dst_ref=x_prev.at[d], send_sem=x_send.at[d], recv_sem=x_recv.at[d],
+            device_id=(q, p + 1, mate(d)), device_id_type=MESH,
+        )
+
+    def send_core():
+        for k in range(CHUNKS):
+            core_copy(k).start()
+
+    def receive_sketch(which):
+        for d in range(n_split):
+            sketch_copy(which, d).wait_recv()
+        total = s_in[which, 0]
+        for d in range(1, n_split):
+            total = total + s_in[which, d]
+        s_in[which, 0] = total
+
+    def send_sketch():
         for which in (1, 0):
             for d in range(n_split):
                 sketch_copy(which, d).start()
@@ -208,16 +226,15 @@
             receive_sketch(0)
         y_buf[...] = dot(c_own[...].reshape(flat), s_in[0, 0]).reshape(c_own.shape)
         if first:
+            for k in range(CHUNKS // 2):
+                core_copy(k).wait_send()
+            pass_turn()
             receive_sketch(1)
         oth_in = s_in[1, 0]
         gram = jnp.zeros((rank, rank), jnp.float32)
         for k in range(CHUNKS):
             rows = pl.ds(k * part, part)
             if first:
-                if k == CHUNKS - 1:
-                    for m in range(CHUNKS - 1):
-                        core_copy(m).wait_send()
-                    pass_turn()
                 core_copy(k).wait_recv()
             oth = c_oth[rows].reshape(part * modes, rank)
             image = y_buf[rows].reshape(part * modes, rank) + dot(oth, oth_in)
@@ -229,7 +246,8 @@
         for d in range(n_split):
             gram_on_copy(d).start()
         if first:
-            core_copy(CHUNKS - 1).wait_send()
+            for k in range(CHUNKS // 2, CHUNKS):
+                core_copy(k).wait_send()
         image = y_buf[...].reshape(flat)
         x_part[:, :rank] = dot(image, c_own[...].reshape(flat), ((0,), (0,)))
         x_part[:, rank:] = dot(image, c_oth[...].reshape(flat), ((0,), (0,)))
@@ -240,7 +258,7 @@
             gram_copy(d).wait_recv()
             total = total + g_in[d - 1]
         inverse = factor(total)
-        ortho = dot(image, inverse * scale, ((1,), (1,)))
+        ortho = dot(image, inverse, ((1,), (1,)))
         out_ref[...] = ortho.reshape(rank, modes, rank)
         for d in range(1, n_split):
             gram_copy(d).wait_send()
@@ -260,7 +278,8 @@
         def _():
             receive_sketch(0)
             receive_sketch(1)
-            send_sketch(False)
+            make_sketch(False)
+            send_sketch()
             pl.semaphore_wait(go_sem, 1)
             send_core()
             for k in range(CHUNKS):
@@ -277,10 +296,10 @@
 
     @pl.when(p == last)
     def _():
-        send_sketch(True)
+        send_sketch()
         pl.semaphore_wait(go_sem, 1)
         send_core()
-        carry = carry_of_previous() * scale
+        carry = carry_of_previous()
         finish_sketch()
         top = jnp.concatenate([c_own[:, i, :] for i in range(modes)], axis=1)
         moved = dot(carry[:, :rank], top)
@@ -303,7 +322,7 @@
     vmem = lambda *shape: pltpu.VMEM(shape, jnp.float32)
     sems = lambda *shape: pltpu.SemaphoreType.DMA(shape)
     out = pl.pallas_call(
-        functools.partial(kernel, n_pair, depth, n_split, n_pair // 4, scale),
+        functools.partial(kernel, n_pair, depth, n_split, n_pair // 4),
         out_shape=jax.ShapeDtypeStruct(own_core.shape, jnp.float32),
         in_specs=[pl.BlockSpec(memory_space=pltpu.HBM)] * 2,
         out_specs=pl.BlockSpec(memory_space=pltpu.VMEM),
@@ -326,7 +345,7 @@
             collective_id=0, has_side_effects=True, vmem_limit_bytes=65000 * 1024
         ),
     )(own_core, sketch_core)
-    return out[None, None]
+    return (out * scale)[None, None]
 
 
 def solution(mesh):

time: 26.8 us -> 27 us (level)
  other arithmetic: 0 us -> 1.88 us
  local copies, waits for them, and re-layouts: 1.87 us -> 0 us
    broadcast_in_dim x0 -> x1, other arithmetic: none -> 1.88 us  [body(): return (out * scale)[None, None]]
    unnamed x1 -> x0, local copies, waits for them, and re-layouts: 1.87 us -> none
where the time goes in v4:
time: 27 us; the launch traced here: 26.9 us
  Pallas kernels  25 us (93%)
  other arithmetic  1.88 us (7%)
    pallas_call x1, Pallas kernels, body(): pl.pallas_call(functools.partial(kernel, n_pair, depth, n_split, n_pair /...  25 us
    broadcast_in_dim x1, other arithmetic, body(): return (out * scale)[None, None]  1.88 us

profile of v4, /device:TPU:27, one launch (start us, length us, event | category | flops | bytes accessed | tf_op | source)
XLA Modules:
  0.0 26.9 jit_solution(10593257776538639855)
XLA Ops:
  0.0 25.0 %shard_map.28 = f32[128,8,128]{2,1,0:T(8,128)} custom-call(f32[128,8,128]{2,1,0:T(8,128)} %bitcast.4, bf16[128,8,128]{2,1,0:T(8,128)(2,1)} %bitcast.5), custom_call_target="tpu_custom_call" | custom-call | tf_op jit(solution)/shard_map/pallas_call | solution.py:324
  25.0 1.9 %multiply_bitcast_fusion = f32[1,1,128,8,128]{4,3,2,1,0:T(8,128)} fusion(f32[128,8,128]{2,1,0:T(8,128)} %shard_map.28), kind=kLoop, calls=%fused_computation | loop fusion | flops 131072 | bytes 1048576 | tf_op jit(solution)/shard_map/broadcast_in_dim | solution.py:348

commit v5 on v4

--- a/solution.py
+++ b/solution.py
@@ -226,15 +226,16 @@
             receive_sketch(0)
         y_buf[...] = dot(c_own[...].reshape(flat), s_in[0, 0]).reshape(c_own.shape)
         if first:
-            for k in range(CHUNKS // 2):
-                core_copy(k).wait_send()
-            pass_turn()
             receive_sketch(1)
         oth_in = s_in[1, 0]
         gram = jnp.zeros((rank, rank), jnp.float32)
         for k in range(CHUNKS):
             rows = pl.ds(k * part, part)
             if first:
+                if k == CHUNKS - 1:
+                    for m in range(CHUNKS - 1):
+                        core_copy(m).wait_send()
+                    pass_turn()
                 core_copy(k).wait_recv()
             oth = c_oth[rows].reshape(part * modes, rank)
             image = y_buf[rows].reshape(part * modes, rank) + dot(oth, oth_in)
@@ -246,8 +247,7 @@
         for d in range(n_split):
             gram_on_copy(d).start()
         if first:
-            for k in range(CHUNKS // 2, CHUNKS):
-                core_copy(k).wait_send()
+            core_copy(CHUNKS - 1).wait_send()
         image = y_buf[...].reshape(flat)
         x_part[:, :rank] = dot(image, c_own[...].reshape(flat), ((0,), (0,)))
         x_part[:, rank:] = dot(image, c_oth[...].reshape(flat), ((0,), (0,)))

time: 27 us -> 25.7 us (0.952)
  Pallas kernels: 25 us -> 23.5 us
    pallas_call x1, Pallas kernels: 25 us -> 23.5 us  [body(): pl.pallas_call(functools.partial(kernel, n_pair, depth, n_split, n_pair /...]
where the time goes in v5:
time: 25.7 us; the launch traced here: 25.3 us
  Pallas kernels  23.5 us (91%)
  other arithmetic  1.88 us (7%)
    pallas_call x1, Pallas kernels, body(): pl.pallas_call(functools.partial(kernel, n_pair, depth, n_split, n_pair /...  23.5 us
    broadcast_in_dim x1, other arithmetic, body(): return (out * scale)[None, None]  1.88 us

profile of v5, /device:TPU:27, one launch (start us, length us, event | category | flops | bytes accessed | tf_op | source)
XLA Modules:
  0.0 25.3 jit_solution(565414215650979749)
XLA Ops:
  0.0 23.5 %shard_map.28 = f32[128,8,128]{2,1,0:T(8,128)} custom-call(f32[128,8,128]{2,1,0:T(8,128)} %bitcast.4, bf16[128,8,128]{2,1,0:T(8,128)(2,1)} %bitcast.5), custom_call_target="tpu_custom_call" | custom-call | tf_op jit(solution)/shard_map/pallas_call | solution.py:324
  23.5 1.9 %multiply_bitcast_fusion = f32[1,1,128,8,128]{4,3,2,1,0:T(8,128)} fusion(f32[128,8,128]{2,1,0:T(8,128)} %shard_map.28), kind=kLoop, calls=%fused_computation | loop fusion | flops 131072 | bytes 1048576 | tf_op jit(solution)/shard_map/broadcast_in_dim | solution.py:348
